TPU v7x, 32 devices: a whole 2x2x4 slice. The times are simulated.
32 devices in a mesh: adapter: 4 (over z), mp: 8 (over y, x, core).
Axes of the slice: x: 2, y: 2, z: 4, core: 2. Of those that a mesh axis runs over, the one named last changes fastest.
Arguments:
- tokens: bfloat16 [1536, 8192], P('adapter', 'mp'), may hold values from -6 to 6
- cotangent: bfloat16 [1536, 1024], P('adapter', 'mp'), may hold values from -6 to 6
- value_weight: bfloat16 [8192, 1024], P('mp', 'adapter'), may hold values from -0.0625 to 0.0625
- down_store: bfloat16 [8, 8, 1024, 64], P(None, 'mp', 'adapter'), may hold values from -0.0625 to 0.0625
- down_first: float32 [8, 8, 1024, 64], P(None, 'mp', 'adapter'), may hold values from -4 to 4
- down_second: float32 [8, 8, 1024, 64], P(None, 'mp', 'adapter'), may hold values from 0.01 to 1
- up_store: bfloat16 [8, 64, 1024], P(None, 'adapter', 'mp'), may hold values from -0.75 to 0.75
- up_first: float32 [8, 64, 1024], P(None, 'adapter', 'mp'), may hold values from -4 to 4
- up_second: float32 [8, 64, 1024], P(None, 'adapter', 'mp'), may hold values from 0.01 to 1
- tile_adapter: int32 [12], replicated, may hold values from 0 to 7
- tile_length: int32 [12], replicated, may hold values from 1 to 128, as said below
- adapter_slot: int32 [8], replicated, may hold values from 0 to 7, each once
Outputs:
- projected: bfloat16 [1536, 1024], P('adapter', 'mp')
- token_gradient: bfloat16 [1536, 8192], P('adapter', 'mp')
- new_down: float32 [8, 8, 1024, 64], P(None, 'mp', 'adapter')
- new_down_first: float32 [8, 8, 1024, 64], P(None, 'mp', 'adapter')
- new_down_second: float32 [8, 8, 1024, 64], P(None, 'mp', 'adapter')
- new_up: float32 [8, 64, 1024], P(None, 'adapter', 'mp')
- new_up_first: float32 [8, 64, 1024], P(None, 'adapter', 'mp')
- new_up_second: float32 [8, 64, 1024], P(None, 'adapter', 'mp')
Inputs may be any that keep to these rules, and one draw needn't show every extreme that they name: `tile_length`: some tile is full in every draw. `adapter_slot`: each slot holds exactly one adapter.
All inputs are finite; a program needn't handle non-finite values.
Results may differ from a plain program's by a relative error of at most 0.0046.
Values may be sent and summed in bfloat16 or wider, within the bound.
A program may use at most 64 MiB of HBM per device.

v0:
```python
import jax
import jax.numpy as jnp
from jax import lax
from jax.sharding import PartitionSpec as P

TILE = 128
STEP = 100


adapter_scale = 2.0
learn_rate = 0.001
beta_one = 0.9
beta_two = 0.999
adam_eps = 1e-08


def adam_step(store, first, second, gradient):
    new_first = beta_one * first + (1.0 - beta_one) * gradient
    new_second = beta_two * second + (1.0 - beta_two) * gradient * gradient
    corr_one = 1.0 - beta_one**STEP
    corr_two = 1.0 - beta_two**STEP
    moved = store.astype(jnp.float32) - learn_rate * (new_first / corr_one) / (
        jnp.sqrt(new_second / corr_two) + adam_eps
    )
    return (moved, new_first, new_second)


def shards(
    tokens,
    cotangent,
    value_weight,
    down_store,
    down_first,
    down_second,
    up_store,
    up_first,
    up_second,
    tile_adapter,
    tile_length,
    adapter_slot,
):
    tile_total = tile_adapter.shape[0]
    tok_count, feat_part = tokens.shape
    head_cols = cotangent.shape[1]
    tiles_here = tok_count // TILE
    adapter_count = adapter_slot.shape[0]
    my_index = lax.axis_index("adapter")
    adapter_ids = jnp.arange(adapter_count, dtype=jnp.int32)
    tile_adapter_slot = jnp.sum(
        jnp.where(tile_adapter[:, None] == adapter_ids[None, :], adapter_slot[None, :], 0), axis=1
    )
    my_lengths = lax.dynamic_slice_in_dim(tile_length, my_index * tiles_here, tiles_here)
    active_rows = (jnp.arange(TILE)[None, :] < my_lengths[:, None]).reshape(tok_count, 1)
    masked_own = cotangent * active_rows.astype(jnp.bfloat16)
    masked_full = lax.all_gather(masked_own, "mp", axis=1, tiled=True)
    sent_down = down_store[:, 0][tile_adapter_slot]
    sent_up = up_store[tile_adapter_slot]
    down_panel, up_panel = (
        lax.all_to_all(sent_down, "adapter", split_axis=0, concat_axis=1, tiled=True),
        lax.all_to_all(sent_up, "adapter", split_axis=0, concat_axis=1, tiled=True),
    )
    token_tiles = tokens.reshape(tiles_here, TILE, feat_part)
    frozen_part = jnp.dot(
        tokens,
        lax.all_gather(value_weight, "adapter", axis=1, tiled=True),
        preferred_element_type=jnp.float32,
    )
    frozen_local = lax.psum_scatter(frozen_part, "mp", scatter_dimension=1, tiled=True)
    down_part = jnp.einsum(
        "ntd,ndr->ntr", token_tiles, down_panel, preferred_element_type=jnp.float32
    )
    down_sum = lax.psum(down_part, "mp")
    down_portion = down_sum.astype(jnp.bfloat16)
    adapter_term = jnp.einsum(
        "ntr,nrv->ntv", down_portion, up_panel, preferred_element_type=jnp.float32
    ).reshape(tok_count, head_cols)
    projected = (
        (frozen_local + adapter_scale * adapter_term) * active_rows.astype(jnp.float32)
    ).astype(jnp.bfloat16)
    tile_mask = masked_own.reshape(tiles_here, TILE, head_cols)
    backward_piece = adapter_scale * jnp.einsum(
        "ntv,nrv->ntr", tile_mask, up_panel, preferred_element_type=jnp.float32
    )
    backward_portion = lax.psum(backward_piece, "mp").astype(jnp.bfloat16)
    frozen_backward = lax.dot_general(
        masked_full,
        lax.all_gather(value_weight, "adapter", axis=1, tiled=True),
        (((1,), (1,)), ((), ())),
        preferred_element_type=jnp.float32,
    )
    adapter_backward = jnp.einsum(
        "ntr,ndr->ntd", backward_portion, down_panel, preferred_element_type=jnp.float32
    ).reshape(tok_count, feat_part)
    token_gradient = (frozen_backward + adapter_backward).astype(jnp.bfloat16)
    home_down = jnp.einsum(
        "ntd,ntr->ndr", token_tiles, backward_portion, preferred_element_type=jnp.float32
    )
    local_up_weight = adapter_scale * jnp.einsum(
        "ntr,ntv->nrv", down_portion, tile_mask, preferred_element_type=jnp.float32
    )
    arrived_down, arrived_up = (
        lax.all_to_all(home_down, "adapter", split_axis=1, concat_axis=0, tiled=True),
        lax.all_to_all(local_up_weight, "adapter", split_axis=1, concat_axis=0, tiled=True),
    )
    selector = (adapter_ids[:, None] == tile_adapter_slot[None, :]).astype(jnp.float32)
    down_gradient = jnp.dot(
        selector, arrived_down.reshape(tile_total, -1), precision=lax.Precision.HIGHEST
    ).reshape(down_store.shape)
    up_gradient = jnp.dot(
        selector, arrived_up.reshape(tile_total, -1), precision=lax.Precision.HIGHEST
    ).reshape(up_store.shape)
    new_down, new_down_first, new_down_second = adam_step(
        down_store, down_first, down_second, down_gradient
    )
    new_up, new_up_first, new_up_second = adam_step(up_store, up_first, up_second, up_gradient)
    return (
        projected,
        token_gradient,
        new_down,
        new_down_first,
        new_down_second,
        new_up,
        new_up_first,
        new_up_second,
    )


def solution(mesh):
    placed = (
        P("adapter", "mp"),
        P("adapter", "mp"),
        P("mp", "adapter"),
        P(None, "mp", "adapter", None),
        P(None, "mp", "adapter", None),
        P(None, "mp", "adapter", None),
        P(None, "adapter", "mp"),
        P(None, "adapter", "mp"),
        P(None, "adapter", "mp"),
        P(),
        P(),
        P(),
    )
    return jax.shard_map(
        shards,
        mesh=mesh,
        in_specs=placed,
        out_specs=(
            P("adapter", "mp"),
            P("adapter", "mp"),
            P(None, "mp", "adapter", None),
            P(None, "mp", "adapter", None),
            P(None, "mp", "adapter", None),
            P(None, "adapter", "mp"),
            P(None, "adapter", "mp"),
            P(None, "adapter", "mp"),
        ),
        check_vma=False,
    )
```

profile of v0, /device:TPU:7, one launch (start us, length us, event | category | flops | bytes accessed | tf_op | source)
XLA Modules:
  0.0 137.0 jit_solution(8212307824235022589)
XLA Ops:
  7.2 0.0 copy-start
  7.2 0.0 copy-start.15
  7.2 0.0 copy-start.8
  7.2 0.0 all-gather.2.cloned.1.call-start
  7.2 0.7 all-gather.2.cloned.1.call-update
  7.9 0.8 select_reduce_fusion
  8.7 0.5 copy-done.11
  9.2 1.9 %gather_fusion.1 = bf16[12,16,128]{2,1,0:T(8,128)(2,1)} fusion(bf16[8,16,128]{2,1,0:T(8,128)(2,1)} %param.18, s32[1024]{0:T(1024)S(1)} %pad_clamp_fusion), kind=kCustom, calls=%fused_computation.1 | custom fusion | bytes 98352 | tf_op jit(solution)/shard_map/gather | solution.py:57
  11.2 4.6 %all-to-all-start.1 = ((bf16[12,16,128]{2,1,0:T(8,128)(2,1)}), bf16[12,16,128]{2,1,0:T(8,128)(2,1)S(1)}, u32[]{:S(2)}, u32[]{:S(2)}) async-start(bf16[12,16,128]{2,1,0:T(8,128)(2,1)} %gather_fusion.1), calls=%async_computation.2 | async-start | bytes 98304 | tf_op jit(solution)/shard_map/all_to_all | solution.py:60
  15.7 2.3 %gather_fusion = bf16[12,256,64]{1,2,0:T(8,128)(2,1)} fusion(bf16[8,256,64]{1,2,0:T(8,128)(2,1)} %bitcast.85, s32[1024]{0:T(1024)S(1)} %pad_clamp_fusion), kind=kCustom, calls=%fused_computation | custom fusion | bytes 786480 | tf_op jit(solution)/shard_map/gather | solution.py:56
  18.0 0.0 copy-done.15
  18.0 0.1 dynamic_slice.3
  18.1 2.2 %all-to-all-done.1 = bf16[12,16,128]{2,1,0:T(8,128)(2,1)S(1)} async-done(((bf16[12,16,128]{2,1,0:T(8,128)(2,1)}), bf16[12,16,128]{2,1,0:T(8,128)(2,1)S(1)}, u32[]{:S(2)}, u32[]{:S(2)}) %all-to-all-start.1) | async-done | bytes 49184 | tf_op jit(solution)/shard_map/all_to_all | solution.py:60
  20.3 3.5 %all-to-all-start = ((bf16[12,256,64]{1,2,0:T(8,128)(2,1)}), bf16[12,256,64]{1,2,0:T(8,128)(2,1)S(1)}, u32[]{:S(2)}, u32[]{:S(2)}) async-start(bf16[12,256,64]{1,2,0:T(8,128)(2,1)} %gather_fusion), calls=%async_computation.1 | async-start | bytes 786432 | tf_op jit(solution)/shard_map/all_to_all | solution.py:59
  23.8 0.6 convert_bitcast_fusion
  24.4 0.0 copy-done.8
  24.4 0.1 broadcast_multiply_fusion
  24.6 0.2 convolution_multiply_fusion.2
  24.7 22.5 %all-to-all-done = bf16[12,256,64]{1,2,0:T(8,128)(2,1)S(1)} async-done(((bf16[12,256,64]{1,2,0:T(8,128)(2,1)}), bf16[12,256,64]{1,2,0:T(8,128)(2,1)S(1)}, u32[]{:S(2)}, u32[]{:S(2)}) %all-to-all-start) | async-done | bytes 393248 | tf_op jit(solution)/shard_map/all_to_all | solution.py:59
  47.2 0.3 copy.120
  47.5 0.3 all_to_all.51
  47.8 0.0 copy-done
  47.8 0.4 convolution_bitcast_fusion.1
  48.2 24.8 %all-reduce.2 = (bf16[3,128,64]{1,2,0:T(8,128)(2,1)S(1)}, bf16[3,128,64]{1,2,0:T(8,128)(2,1)S(1)}) all-reduce(f32[3,128,64]{1,2,0:T(8,128)S(1)} %convolution_bitcast_fusion.1, f32[3,128,64]{1,2,0:T(8,128)S(1)} %convolution_multiply_fusion.2), channel_id=1, replica_groups=mesh['adapter'=4,'mp'=8] {'mp'}, use_global_device_ids=true, to_apply=%region_2.3 | all-reduce | flops 49152 | bytes 294912 | tf_op jit(solution)/shard_map/psum | solution.py:72
  73.0 0.0 copy-start.6
  73.0 0.0 copy-start.4
  73.0 0.1 convolution_multiply_fusion.1
  73.1 0.7 copy.95
  73.9 3.3 %all-to-all-start.3 = ((f32[3,64,128]{2,0,1:T(4,128)}), f32[3,64,128]{2,0,1:T(4,128)S(1)}, u32[]{:S(2)}, u32[]{:S(2)}) async-start(f32[3,64,128]{2,0,1:T(4,128)} %copy.95), calls=%async_computation.4 | async-start | bytes 262144 | tf_op jit(solution)/shard_map/all_to_all | solution.py:103
  77.2 0.0 reduce-scatter.2.cloned.1.call-start
  77.2 0.0 all-gather.2.cloned.1.call-done
  77.3 3.7 %fusion.24 = f32[384,1024]{1,0:T(8,128)} fusion(bf16[384,1024]{1,0:T(8,128)(2,1)S(1)} %copy-done, bf16[1024,1024]{1,0:T(8,128)(2,1)} %all-gather.2.cloned.1.call-done), kind=kOutput, calls=%fused_computation.47 | convolution fusion | flops 805306368 | bytes 4456448 | tf_op jit(solution)/shard_map/dot_general | solution.py:63
  81.0 0.0 copy-done.6
  81.0 0.0 reduce-scatter.2.cloned.1.call-update
  81.0 0.0 copy-done.4
  81.0 1.1 convolution_bitcast_fusion
  82.2 1.8 %copy.88 = f32[3,1024,64]{2,0,1:T(4,128)S(1)} copy(f32[3,1024,64]{1,2,0:T(8,128)} %convolution_bitcast_fusion) | data formatting | bytes 1572864 | tf_op jit(solution)/shard_map/ntd,ntr->ndr/dot_general | solution.py:95
  84.0 2.6 %reshape.150 = f32[4,1,49152]{2,1,0:T(1,128)} reshape(f32[1024,3,64]{2,1,0:T(4,128)S(1)} %bitcast.83) | data formatting | bytes 1572864
  86.6 0.0 all-to-all-done.3
  86.6 4.6 %all-to-all-start.2 = ((f32[4,1,49152]{2,1,0:T(1,128)}), f32[4,1,49152]{2,1,0:T(1,128)S(1)}, u32[]{:S(2)}, u32[]{:S(2)}) async-start(f32[4,1,49152]{2,1,0:T(1,128)} %reshape.150), calls=%async_computation.3 | async-start | bytes 1572864 | tf_op jit(solution)/shard_map/all_to_all | solution.py:102
  91.1 0.0 copy-start.14
  91.2 13.0 %all_gather.8 = bf16[384,1024]{1,0:T(8,128)(2,1)} all-gather(bf16[384,128]{1,0:T(8,128)(2,1)S(1)} %broadcast_multiply_fusion), channel_id=1, replica_groups=mesh['adapter'=4,'mp'=8] {'mp'}, dimensions={1}, use_global_device_ids=true | all-gather | bytes 884736 | tf_op jit(solution)/shard_map/all_gather | solution.py:55
  104.1 0.0 copy-done.7
  104.1 0.2 convolution_multiply_fusion
  104.4 0.0 copy-done.5
  104.4 1.6 %fusion.25 = f32[3,128,1024]{2,1,0:T(8,128)} fusion(bf16[3,128,64]{1,2,0:T(8,128)(2,1)S(1)} %copy-done.5, bf16[3,1024,64]{1,2,0:T(8,128)(2,1)S(1)} %all_to_all.51), kind=kOutput, calls=%fused_computation.48 | convolution fusion | flops 50331648 | bytes 2015232 | tf_op jit(solution)/shard_map/ntr,ndr->ntd/dot_general | solution.py:91
  106.0 0.2 divide_subtract_fusion.1
  106.2 0.6 copy.100
  106.9 0.6 copy.101
  107.5 0.6 copy.99
  108.2 3.0 %all-to-all-done.2 = f32[4,1,49152]{2,1,0:T(1,128)S(1)} async-done(((f32[4,1,49152]{2,1,0:T(1,128)}), f32[4,1,49152]{2,1,0:T(1,128)S(1)}, u32[]{:S(2)}, u32[]{:S(2)}) %all-to-all-start.2) | async-done | bytes 786464 | tf_op jit(solution)/shard_map/all_to_all | solution.py:102
  111.1 0.5 broadcast.74
  111.7 3.8 %reduce = f32[4,49152]{1,0:T(4,128)} reduce(f32[4,1,49152]{2,1,0:T(1,128)S(1)} %all-to-all-done.2, f32[]{:T(128)} %broadcast.74), dimensions={1}, to_apply=%all_to_all.56.reduce_sub_computation | reduce | bytes 1572868 | tf_op jit(solution)/shard_map/all_to_all | solution.py:102
  115.5 2.3 %reshape.151 = f32[1024,3,64]{2,1,0:T(4,128)S(1)} reshape(f32[4,49152]{1,0:T(4,128)} %reduce) | data formatting | bytes 1572864
  117.8 1.3 copy.119
  119.1 1.9 %reshape.128 = f32[12,16384]{1,0:T(8,128)S(1)} reshape(f32[4,3,256,64]{3,2,1,0:T(8,128)} %bitcast.84) | data formatting | bytes 1572864 | tf_op jit(solution)/shard_map/reshape | solution.py:107
  121.0 0.5 fusion.14
  121.5 0.4 reshape.129
  121.9 0.3 copy.90
  122.3 2.7 %divide_subtract_fusion = (f32[8,1,256,64]{2,3,1,0:T(8,128)}, f32[8,1,256,64]{2,3,1,0:T(8,128)}, f32[8,1,256,64]{2,3,1,0:T(8,128)}) fusion(bf16[8,1,256,64]{2,3,1,0:T(8,128)(2,1)S(1)} %copy-done.1, f32[8,1,256,64]{2,3,1,0:T(8,128)S(1)} %copy.90, f32[8,1,256,64]{2,3,1,0:T(8,128)} %param.16, f32[8,1,256,64]{2,3,1,0:T(8,128)} %param.17), kind=kLoop, calls=%fused_computation.12 | loop fusion | flops 1703936 | bytes 3407872 | tf_op jit(solution)/shard_map/sub | solution.py:22
  125.0 0.0 copy-done.3
  125.0 3.5 %fusion = bf16[384,1024]{1,0:T(8,128)(2,1)} fusion(f32[3,128,1024]{2,1,0:T(8,128)S(1)} %copy-done.2, bf16[384,1024]{1,0:T(8,128)(2,1)S(1)} %copy-done.3, bf16[1024,1024]{1,0:T(8,128)(2,1)} %all-gather.2.cloned.1.call-done), kind=kOutput, calls=%fused_computation.3 | convolution fusion | flops 806092800 | bytes 5242880 | tf_op jit(solution)/shard_map/dot_general | solution.py:85
  128.5 0.0 copy-done.10
  128.5 1.7 %fusion.3 = bf16[384,128]{1,0:T(8,128)(2,1)} fusion(f32[384,128]{1,0:T(8,128)} %reduce-scatter.2.cloned.1.call-done, f32[3,128,128]{2,1,0:T(8,128)S(1)} %convolution_multiply_fusion, f32[384]{0:T(512)S(1)} %copy-done.10), kind=kLoop, calls=%fused_computation.17 | loop fusion | flops 147456 | bytes 493056 | tf_op jit(solution)/shard_map/convert_element_type | solution.py:79
  (22 shorter events, 0.1 us)
Async XLA Ops:
  7.2 40.6 %copy-start = (bf16[384,1024]{1,0:T(8,128)(2,1)S(1)}, bf16[384,1024]{1,0:T(8,128)(2,1)}, u32[]{:S(2)}) copy-start(bf16[384,1024]{1,0:T(8,128)(2,1)} %param.12) | copy-start | bytes 2359300
  7.2 10.8 %copy-start.15 = (s32[12]{0:T(128)S(1)}, s32[12]{0:T(128)}, u32[]{:S(2)}) copy-start(s32[12]{0:T(128)} %param.22) | copy-start | bytes 148
  7.2 17.2 %copy-start.8 = (bf16[384,128]{1,0:T(8,128)(2,1)S(1)}, bf16[384,128]{1,0:T(8,128)(2,1)}, u32[]{:S(2)}) copy-start(bf16[384,128]{1,0:T(8,128)(2,1)} %param.13) | copy-start | bytes 294916
  7.2 70.1 %all-gather.2.cloned.1.call-start = ((), (), s32[]{:S(2)}) async-start(), calls=%async_computation.5 | async-start | bytes 2621440 | tf_op jit(solution)/shard_map/all_gather | solution.py:65
  8.7 0.5 copy-start.11
  11.2 9.1 %all-to-all-start.1 = ((bf16[12,16,128]{2,1,0:T(8,128)(2,1)}), bf16[12,16,128]{2,1,0:T(8,128)(2,1)S(1)}, u32[]{:S(2)}, u32[]{:S(2)}) async-start(bf16[12,16,128]{2,1,0:T(8,128)(2,1)} %gather_fusion.1), calls=%async_computation.2 | async-start | bytes 98304 | tf_op jit(solution)/shard_map/all_to_all | solution.py:60
  20.3 26.9 %all-to-all-start = ((bf16[12,256,64]{1,2,0:T(8,128)(2,1)}), bf16[12,256,64]{1,2,0:T(8,128)(2,1)S(1)}, u32[]{:S(2)}, u32[]{:S(2)}) async-start(bf16[12,256,64]{1,2,0:T(8,128)(2,1)} %gather_fusion), calls=%async_computation.1 | async-start | bytes 786432 | tf_op jit(solution)/shard_map/all_to_all | solution.py:59
  73.0 8.0 %copy-start.6 = (bf16[3,128,64]{1,2,0:T(8,128)(2,1)}, bf16[3,128,64]{1,2,0:T(8,128)(2,1)S(1)}, u32[]{:S(2)}) copy-start(bf16[3,128,64]{1,2,0:T(8,128)(2,1)S(1)} %get-tuple-element.48) | copy-start | bytes 147460
  73.0 8.1 %copy-start.4 = (bf16[3,128,64]{1,2,0:T(8,128)(2,1)}, bf16[3,128,64]{1,2,0:T(8,128)(2,1)S(1)}, u32[]{:S(2)}) copy-start(bf16[3,128,64]{1,2,0:T(8,128)(2,1)S(1)} %get-tuple-element.49) | copy-start | bytes 147460
  73.9 12.7 %all-to-all-start.3 = ((f32[3,64,128]{2,0,1:T(4,128)}), f32[3,64,128]{2,0,1:T(4,128)S(1)}, u32[]{:S(2)}, u32[]{:S(2)}) async-start(f32[3,64,128]{2,0,1:T(4,128)} %copy.95), calls=%async_computation.4 | async-start | bytes 262144 | tf_op jit(solution)/shard_map/all_to_all | solution.py:103
  77.2 51.3 %reduce-scatter.2.cloned.1.call-start = ((), (), s32[]{:S(2)}) async-start(), calls=%async_computation.6 | async-start | bytes 1769472 | tf_op jit(solution)/shard_map/reduce_scatter | solution.py:68
  86.6 17.6 %copy-start.7 = (bf16[3,128,64]{1,2,0:T(8,128)(2,1)S(1)}, bf16[3,128,64]{1,2,0:T(8,128)(2,1)}, u32[]{:S(2)}) copy-start(bf16[3,128,64]{1,2,0:T(8,128)(2,1)} %copy-done.6) | copy-start | bytes 147460
  86.6 17.8 %copy-start.5 = (bf16[3,128,64]{1,2,0:T(8,128)(2,1)S(1)}, bf16[3,128,64]{1,2,0:T(8,128)(2,1)}, u32[]{:S(2)}) copy-start(bf16[3,128,64]{1,2,0:T(8,128)(2,1)} %copy-done.4) | copy-start | bytes 147460
  86.6 24.6 %all-to-all-start.2 = ((f32[4,1,49152]{2,1,0:T(1,128)}), f32[4,1,49152]{2,1,0:T(1,128)S(1)}, u32[]{:S(2)}, u32[]{:S(2)}) async-start(f32[4,1,49152]{2,1,0:T(1,128)} %reshape.150), calls=%async_computation.3 | async-start | bytes 1572864 | tf_op jit(solution)/shard_map/all_to_all | solution.py:102
  91.1 14.8 %copy-start.9 = (bf16[8,16,128]{2,1,0:T(8,128)(2,1)S(1)}, bf16[8,16,128]{2,1,0:T(8,128)(2,1)}, u32[]{:S(2)}) copy-start(bf16[8,16,128]{2,1,0:T(8,128)(2,1)} %param.18) | copy-start | bytes 98308
  91.1 14.8 %copy-start.12 = (s32[12]{0:T(128)S(1)}, s32[12]{0:T(128)}, u32[]{:S(2)}) copy-start(s32[12]{0:T(128)} %copy-done.11) | copy-start | bytes 148
  91.1 14.8 %copy-start.13 = (f32[8,16,128]{2,1,0:T(8,128)S(1)}, f32[8,16,128]{2,1,0:T(8,128)}, u32[]{:S(2)}) copy-start(f32[8,16,128]{2,1,0:T(8,128)} %param.19) | copy-start | bytes 196612
  91.1 14.8 %copy-start.14 = (f32[8,16,128]{2,1,0:T(8,128)S(1)}, f32[8,16,128]{2,1,0:T(8,128)}, u32[]{:S(2)}) copy-start(f32[8,16,128]{2,1,0:T(8,128)} %param.20) | copy-start | bytes 196612
  121.0 1.2 copy-start.1
  122.3 2.7 %copy-start.2 = (f32[3,128,1024]{2,1,0:T(8,128)S(1)}, f32[3,128,1024]{2,1,0:T(8,128)}, u32[]{:S(2)}) copy-start(f32[3,128,1024]{2,1,0:T(8,128)} %fusion.25) | copy-start | bytes 4718596
  122.3 2.7 %copy-start.3 = (bf16[384,1024]{1,0:T(8,128)(2,1)S(1)}, bf16[384,1024]{1,0:T(8,128)(2,1)}, u32[]{:S(2)}) copy-start(bf16[384,1024]{1,0:T(8,128)(2,1)} %all_gather.8) | copy-start | bytes 2359300
  125.0 3.5 %copy-start.10 = (f32[384]{0:T(512)S(1)}, f32[384]{0:T(512)}, u32[]{:S(2)}) copy-start(f32[384]{0:T(512)} %get-tuple-element.56) | copy-start | bytes 4612
Sparse Core Ops, SparseCore 0:
  9.6 57.7 all-gather.1
  81.3 39.0 reduce-scatter.1
where the time goes:
time: 139 us; the launch traced here: 137 us
  blocking collectives  37.7 us (27%)
  waiting for transfers between devices  28.4 us (20%)
  local copies, waits for them, and re-layouts  19.3 us (14%)
  starting transfers between devices  16 us (12%)
  between operations  14.3 us (10%)
  matrix products  11.6 us (8%)
  other arithmetic  9.71 us (7%)
    psum x1, blocking collectives, shards(): down_sum = lax.psum(down_part, 'mp')  24.8 us
    all_to_all x1, waiting for transfers between devices, shards(): lax.all_to_all(sent_down, 'adapter', split_axis=0, concat_axis=1, tiled=T...  22.5 us
    all_gather x1, blocking collectives, shards(): masked_full = lax.all_gather(masked_own, 'mp', axis=1, tiled=True)  13 us
    unnamed x37, local copies, waits for them, and re-layouts  7.39 us
    all_to_all x1, starting transfers between devices, shards(): lax.all_to_all(sent_up, 'adapter', split_axis=0, concat_axis=1, tiled=True)  4.59 us
    all_to_all x1, starting transfers between devices, shards(): lax.all_to_all(home_down, 'adapter', split_axis=1, concat_axis=0, tiled=T...  4.57 us
    all_to_all x1, other arithmetic, shards(): lax.all_to_all(home_down, 'adapter', split_axis=1, concat_axis=0, tiled=T...  3.79 us
    dot_general x1, matrix products, shards(): jnp.dot(tokens, lax.all_gather(value_weight, 'adapter', axis=1, tiled=Tru...  3.72 us
  transfers between devices with their start and end apart: 6, of which 3 were waited for; matrix products, arithmetic and copies ran while one was open for 28% of the time, Pallas kernels for 0%

commit v1 on v0

--- a/solution.py
+++ b/solution.py
@@ -1,6 +1,10 @@
+import functools
+
 import jax
 import jax.numpy as jnp
 from jax import lax
+from jax.experimental import pallas as pl
+from jax.experimental.pallas import tpu as pltpu
 from jax.sharding import PartitionSpec as P
 
 TILE = 128
@@ -125,6 +129,445 @@
     )
 
 
+F32 = jnp.float32
+BF16 = jnp.bfloat16
+NT = (((1,), (1,)), ((), ()))
+TN = (((0,), (0,)), ((), ()))
+
+
+def dot(a, b, dims=(((1,), (0,)), ((), ()))):
+    return lax.dot_general(a, b, dims, preferred_element_type=F32)
+
+
+def fused_kernel(
+    na,
+    nm,
+    tad,
+    tlen,
+    aslot,
+    tok,
+    cot,
+    w,
+    down,
+    up,
+    proj,
+    tgrad,
+    gdown,
+    gup,
+    wbuf,
+    masked,
+    sel_d,
+    sel_u,
+    pan_d,
+    pan_u,
+    part,
+    rs_in,
+    db,
+    term,
+    fro_send,
+    fro_recv,
+    fro_own,
+    acc,
+    g_send,
+    g_recv,
+    gu_send,
+    gu_recv,
+    wr_s,
+    wl_s,
+    w_r,
+    pd_s,
+    pd_r,
+    pu_s,
+    pu_r,
+    ms_s,
+    ms_r,
+    rs_s,
+    rs_r,
+    ag_s,
+    ag_r,
+    fs_s,
+    fs_r,
+    gd_s,
+    gd_r,
+    gu_s,
+    gu_r,
+):
+    z = lax.axis_index("adapter")
+    m = lax.axis_index("mp")
+    cols = cot.shape[1]
+    heads = w.shape[1] // cols
+    tiles = tok.shape[0] // TILE
+    rank = down.shape[1]
+    depth = down.shape[2]
+    rank_part = up.shape[1]
+    slots = down.shape[0]
+    block = tok.shape[0] // nm
+
+    def other_z(d):
+        return lax.rem(z + d, na)
+
+    def other_m(d):
+        return lax.rem(m + d, nm)
+
+    def remote(src, dst, send, recv, device):
+        return pltpu.make_async_remote_copy(
+            src_ref=src,
+            dst_ref=dst,
+            send_sem=send,
+            recv_sem=recv,
+            device_id=device,
+            device_id_type=pl.DeviceIdType.MESH,
+        )
+
+    def to_right(g):
+        return remote(
+            wbuf.at[g], wbuf.at[g], wr_s.at[g], w_r.at[g], {"adapter": lax.rem(z + 1, na)}
+        )
+
+    def to_left(g):
+        return remote(
+            wbuf.at[g], wbuf.at[g], wl_s.at[g], w_r.at[g], {"adapter": lax.rem(z + na - 1, na)}
+        )
+
+    def panel_down(src, dst, to):
+        return remote(sel_d.at[to], pan_d.at[dst], pd_s.at[to], pd_r.at[src], {"adapter": to})
+
+    def panel_up(src, dst, to):
+        return remote(sel_u.at[to], pan_u.at[dst], pu_s.at[to], pu_r.at[src], {"adapter": to})
+
+    def mask_copy(src, to):
+        return remote(masked.at[src], masked.at[src], ms_s.at[to], ms_r.at[src], {"mp": to})
+
+    def sum_copy(src, to):
+        at = pl.ds(pl.multiple_of(to * block, block), block)
+        return remote(part.at[at], rs_in.at[src], rs_s.at[to], rs_r.at[src], {"mp": to})
+
+    def rows_copy(src, to):
+        at = pl.ds(pl.multiple_of(src * block, block), block)
+        return remote(db.at[at], db.at[at], ag_s.at[to], ag_r.at[src], {"mp": to})
+
+    def frozen_copy(src, to):
+        return remote(
+            fro_send.at[to], fro_recv.at[src], fs_s.at[to], fs_r.at[src], {"mp": to}
+        )
+
+    def grad_down_copy(src, to):
+        return remote(g_send.at[to], g_recv.at[src], gd_s.at[to], gd_r.at[src], {"adapter": to})
+
+    def grad_up_copy(src, to):
+        return remote(gu_send.at[to], gu_recv.at[src], gu_s.at[to], gu_r.at[src], {"adapter": to})
+
+    slot_of = [aslot[tad[i]] for i in range(na * tiles)]
+    for i in range(na * tiles):
+        sel_d[i // tiles, i % tiles] = down[slot_of[i]]
+        sel_u[i // tiles, i % tiles] = up[slot_of[i]]
+    pan_d[z] = sel_d[z]
+    pan_u[z] = sel_u[z]
+    for h in range(heads):
+        wbuf[z * heads + h] = w[:, h * cols : (h + 1) * cols]
+
+    def live(n):
+        row = lax.broadcasted_iota(jnp.int32, (TILE, cols), 0)
+        return jnp.where(row < tlen[z * tiles + n], 1.0, 0.0)
+
+    for n in range(tiles):
+        at = slice(n * TILE, (n + 1) * TILE)
+        masked[m, at] = (cot[at].astype(F32) * live(n)).astype(BF16)
+
+    barrier = pltpu.get_barrier_semaphore()
+    for d in range(1, na):
+        pl.semaphore_signal(
+            barrier, inc=1, device_id={"adapter": other_z(d)}, device_id_type=pl.DeviceIdType.MESH
+        )
+    for d in range(1, nm):
+        pl.semaphore_signal(
+            barrier, inc=1, device_id={"mp": other_m(d)}, device_id_type=pl.DeviceIdType.MESH
+        )
+    pl.semaphore_wait(barrier, na + nm - 2)
+
+    for d in range(1, na):
+        panel_up(z, z, other_z(d)).start()
+    for d in range(1, na):
+        panel_down(z, z, other_z(d)).start()
+    for h in range(heads):
+
+        @pl.when(z < na - 1)
+        def _():
+            to_right(z * heads + h).start()
+
+        @pl.when(z > 0)
+        def _():
+            to_left(z * heads + h).start()
+
+    for d in range(1, nm):
+        mask_copy(m, other_m(d)).start()
+
+    for d in range(1, na):
+        panel_up(other_z(d), z, other_z(d)).wait_recv()
+    for d in range(1, na):
+        panel_down(other_z(d), other_z(d), other_z(d)).wait_recv()
+
+    def up_panel(n):
+        return jnp.concatenate([pan_u[j, n] for j in range(na)], axis=0)
+
+    for n in range(tiles):
+        at = slice(n * TILE, (n + 1) * TILE)
+        down_part = dot(tok[at, 0:depth], pan_d[0, n], NT)
+        for j in range(1, na):
+            down_part += dot(tok[at, j * depth : (j + 1) * depth], pan_d[j, n], NT)
+        back_part = adapter_scale * dot(masked[m, at], up_panel(n), NT)
+        part[at] = jnp.concatenate([down_part, back_part], axis=1)
+    for d in range(1, nm):
+        sum_copy(m, other_m(d)).start()
+
+    def forward(g):
+        value = dot(tok[...], wbuf[g])
+
+        @pl.when(g == m)
+        def _():
+            fro_own[...] = value
+
+        @pl.when(g != m)
+        def _():
+            fro_send[g] = value.astype(BF16)
+            frozen_copy(m, g).start()
+
+    def backward(g):
+        acc[...] += dot(masked[g], wbuf[g], NT)
+
+    def own_forward(h, carry):
+        forward(z * heads + h)
+        return carry
+
+    lax.fori_loop(0, heads, own_forward, 0)
+
+    total = part[pl.ds(pl.multiple_of(m * block, block), block)]
+    for d in range(1, nm):
+        sum_copy(other_m(d), other_m(d)).wait_recv()
+        total += rs_in[other_m(d)]
+    db[pl.ds(pl.multiple_of(m * block, block), block)] = total.astype(BF16)
+    for d in range(1, nm):
+        rows_copy(m, other_m(d)).start()
+    for d in range(1, nm):
+        rows_copy(other_m(d), other_m(d)).wait_recv()
+
+    for n in range(tiles):
+        at = slice(n * TILE, (n + 1) * TILE)
+        both = db[at]
+        down_rows, back_rows = both[:, :rank], both[:, rank:]
+        g_tile = dot(back_rows, tok[at], TN)
+        gu_tile = adapter_scale * dot(down_rows, masked[m, at], TN)
+        for j in range(na):
+            g_send[j, n] = g_tile[:, j * depth : (j + 1) * depth].astype(BF16)
+            gu_send[j, n] = gu_tile[j * rank_part : (j + 1) * rank_part]
+    for d in range(1, na):
+        grad_down_copy(z, other_z(d)).start()
+        grad_up_copy(z, other_z(d)).start()
+    g_recv[z] = g_send[z]
+    gu_recv[z] = gu_send[z]
+    for n in range(tiles):
+        at = slice(n * TILE, (n + 1) * TILE)
+        both = db[at]
+        down_rows, back_rows = both[:, :rank], both[:, rank:]
+        term[at] = adapter_scale * dot(down_rows, up_panel(n))
+        for j in range(na):
+            acc[at, j * depth : (j + 1) * depth] = dot(back_rows, pan_d[j, n])
+
+    for d in range(1, nm):
+        mask_copy(other_m(d), other_m(d)).wait_recv()
+
+    def own_backward(h, carry):
+        backward(z * heads + h)
+        return carry
+
+    lax.fori_loop(0, heads, own_backward, 0)
+
+    def relay(t, carry):
+        step = t // heads + 1
+        h = lax.rem(t, heads)
+        lower = (z - step) * heads + h
+        upper = (z + step) * heads + h
+
+        @pl.when(z >= step)
+        def _():
+            to_right(lower).wait_recv()
+
+            @pl.when(z < na - 1)
+            def _():
+                to_right(lower).start()
+
+        @pl.when(z + step < na)
+        def _():
+            to_left(upper).wait_recv()
+
+            @pl.when(z > 0)
+            def _():
+                to_left(upper).start()
+
+        def one(side, inner):
+            head = (z + (2 * side - 1) * step) * heads + h
+            valid = jnp.logical_and(head >= 0, head < na * heads)
+
+            @pl.when(valid)
+            def _():
+                forward(head)
+                backward(head)
+
+            return inner
+
+        return lax.fori_loop(0, 2, one, carry)
+
+    lax.fori_loop(0, (na - 1) * heads, relay, 0)
+
+    for d in range(1, na):
+        grad_down_copy(other_z(d), other_z(d)).wait_recv()
+        grad_up_copy(other_z(d), other_z(d)).wait_recv()
+
+    def slot_sum(s, carry):
+        total_d = jnp.zeros((rank, depth), F32)
+        total_u = jnp.zeros((rank_part, cols), F32)
+        for i in range(na * tiles):
+            use = jnp.where(slot_of[i] == s, 1.0, 0.0)
+            total_d += use * g_recv[i // tiles, i % tiles].astype(F32)
+            total_u += use * gu_recv[i // tiles, i % tiles]
+        gdown[s] = total_d
+        gup[s] = total_u
+        return carry
+
+    lax.fori_loop(0, slots, slot_sum, 0)
+    tgrad[...] = acc[...].astype(BF16)
+
+    for d in range(1, nm):
+        frozen_copy(other_m(d), other_m(d)).wait_recv()
+    for n in range(tiles):
+        at = slice(n * TILE, (n + 1) * TILE)
+        value = fro_own[at] + term[at]
+        for d in range(1, nm):
+            value += fro_recv[other_m(d), at].astype(F32)
+        proj[at] = (value * live(n)).astype(BF16)
+
+    for d in range(1, na):
+        panel_up(z, z, other_z(d)).wait_send()
+        panel_down(z, z, other_z(d)).wait_send()
+        grad_down_copy(z, other_z(d)).wait_send()
+        grad_up_copy(z, other_z(d)).wait_send()
+    for d in range(1, nm):
+        mask_copy(m, other_m(d)).wait_send()
+        sum_copy(m, other_m(d)).wait_send()
+        rows_copy(m, other_m(d)).wait_send()
+        frozen_copy(m, other_m(d)).wait_send()
+
+    def drain(g, carry):
+        owner = g // heads
+
+        @pl.when(jnp.logical_and(owner <= z, z < na - 1))
+        def _():
+            to_right(g).wait_send()
+
+        @pl.when(jnp.logical_and(owner >= z, z > 0))
+        def _():
+            to_left(g).wait_send()
+
+        return carry
+
+    lax.fori_loop(0, na * heads, drain, 0)
+
+
+def fused_shards(
+    na,
+    nm,
+    tokens,
+    cotangent,
+    value_weight,
+    down_store,
+    down_first,
+    down_second,
+    up_store,
+    up_first,
+    up_second,
+    tile_adapter,
+    tile_length,
+    adapter_slot,
+):
+    rows, feats = tokens.shape
+    cols = cotangent.shape[1]
+    tiles = rows // TILE
+    slots, _, depth, rank = down_store.shape
+    part = up_store.shape[1]
+    down_t = jnp.swapaxes(down_store[:, 0], 1, 2)
+    vmem = pl.BlockSpec(memory_space=pltpu.VMEM)
+    smem = pl.BlockSpec(memory_space=pltpu.SMEM)
+    dma = pltpu.SemaphoreType.DMA
+    sds = jax.ShapeDtypeStruct
+    proj, tgrad, gdown, gup = pl.pallas_call(
+        functools.partial(fused_kernel, na, nm),
+        out_shape=(
+            sds((rows, cols), BF16),
+            sds((rows, feats), BF16),
+            sds((slots, rank, depth), F32),
+            sds((slots, part, cols), F32),
+        ),
+        in_specs=[smem] * 3 + [vmem] * 5,
+        out_specs=(vmem,) * 4,
+        scratch_shapes=[
+            pltpu.VMEM((nm, feats, cols), BF16),
+            pltpu.VMEM((nm, rows, cols), BF16),
+            pltpu.VMEM((na, tiles, rank, depth), BF16),
+            pltpu.VMEM((na, tiles, part, cols), BF16),
+            pltpu.VMEM((na, tiles, rank, depth), BF16),
+            pltpu.VMEM((na, tiles, part, cols), BF16),
+            pltpu.VMEM((rows, 2 * rank), F32),
+            pltpu.VMEM((nm, rows // nm, 2 * rank), F32),
+            pltpu.VMEM((rows, 2 * rank), BF16),
+            pltpu.VMEM((rows, cols), F32),
+            pltpu.VMEM((nm, rows, cols), BF16),
+            pltpu.VMEM((nm, rows, cols), BF16),
+            pltpu.VMEM((rows, cols), F32),
+            pltpu.VMEM((rows, feats), F32),
+            pltpu.VMEM((na, tiles, rank, depth), BF16),
+            pltpu.VMEM((na, tiles, rank, depth), BF16),
+            pltpu.VMEM((na, tiles, part, cols), F32),
+            pltpu.VMEM((na, tiles, part, cols), F32),
+            dma((nm,)),
+            dma((nm,)),
+            dma((nm,)),
+            dma((na,)),
+            dma((na,)),
+            dma((na,)),
+            dma((na,)),
+            dma((nm,)),
+            dma((nm,)),
+            dma((nm,)),
+            dma((nm,)),
+            dma((nm,)),
+            dma((nm,)),
+            dma((nm,)),
+            dma((nm,)),
+            dma((na,)),
+            dma((na,)),
+            dma((na,)),
+            dma((na,)),
+        ],
+        compiler_params=pltpu.CompilerParams(
+            collective_id=0, has_side_effects=True, vmem_limit_bytes=40 * 1024 * 1024
+        ),
+    )(tile_adapter, tile_length, adapter_slot, tokens, cotangent, value_weight, down_t, up_store)
+    down_gradient = jnp.swapaxes(gdown, 1, 2)[:, None]
+    return (
+        proj,
+        tgrad,
+        *adam_step(down_store, down_first, down_second, down_gradient),
+        *adam_step(up_store, up_first, up_second, gup),
+    )
+
+
+def by_share(na, nm, *arrays):
+    rows, cols = arrays[1].shape
+    share = arrays[2].shape[1]
+    fits = cols % 128 == 0 and share % cols == 0 and rows % (16 * nm) == 0
+    return fused_shards(na, nm, *arrays) if fits else shards(*arrays)
+
+
 def solution(mesh):
     placed = (
         P("adapter", "mp"),
@@ -141,7 +584,7 @@
         P(),
     )
     return jax.shard_map(
-        shards,
+        functools.partial(by_share, mesh.shape["adapter"], mesh.shape["mp"]),
         mesh=mesh,
         in_specs=placed,
         out_specs=(

time: 139 us -> 76.7 us (0.55); the launches traced: 137 us -> 76.3 us
  Pallas kernels: 0 us -> 66.5 us
  blocking collectives: 37.7 us -> 0 us
  waiting for transfers between devices: 28.4 us -> 0 us
  starting transfers between devices: 16 us -> 0 us
  between operations: 14.3 us -> 0.71 us
  local copies, waits for them, and re-layouts: 19.3 us -> 6.97 us
  matrix products: 11.6 us -> 0 us
  other arithmetic: 9.71 us -> 2.18 us
    pallas_call x0 -> x1, Pallas kernels: none -> 66.5 us  [fused_shards(): pl.pallas_call(functools.partial(fused_kernel, na, nm), out_shape=(sds((r...]
    all_to_all x4 -> x0, waiting for transfers between devices: 27.7 us -> none  [the longest x1 22.5 us: shards(): lax.all_to_all(sent_down, 'adapter', split_axis=0, concat_axis=1, tiled=T...]
    psum x1 -> x0, blocking collectives: 24.8 us -> none  [shards(): down_sum = lax.psum(down_part, 'mp')]
    all_to_all x4 -> x0, starting transfers between devices: 15.9 us -> none  [the longest x1 4.59 us: shards(): lax.all_to_all(sent_up, 'adapter', split_axis=0, concat_axis=1, tiled=True)]
    all_gather x1 -> x0, blocking collectives: 13 us -> none  [shards(): masked_full = lax.all_gather(masked_own, 'mp', axis=1, tiled=True)]
    dot_general x10 -> x0, matrix products: 11.6 us -> none  [the longest x1 3.72 us: shards(): jnp.dot(tokens, lax.all_gather(value_weight, 'adapter', axis=1, tiled=Tru...]
    gather x2 -> x0, local copies, waits for them, and re-layouts: 4.21 us -> none  [the longest x1 2.28 us: shards(): sent_down = down_store[:, 0][tile_adapter_slot]]
    all_to_all x1 -> x0, other arithmetic: 3.79 us -> none  [shards(): lax.all_to_all(home_down, 'adapter', split_axis=1, concat_axis=0, tiled=T...]
  transfers between devices with their start and end apart: 6 -> 0, of which waited for: 3 -> 0; matrix products, arithmetic and copies ran while one was open for 28% -> 0% of each run, Pallas kernels for 0% -> 0%
where the time goes in v1:
time: 76.7 us; the launch traced here: 76.3 us
  Pallas kernels  66.5 us (87%)
  local copies, waits for them, and re-layouts  6.97 us (9%)
  other arithmetic  2.18 us (3%)
    pallas_call x1, Pallas kernels, fused_shards(): pl.pallas_call(functools.partial(fused_kernel, na, nm), out_shape=(sds((r...  66.5 us
    unnamed x26, local copies, waits for them, and re-layouts  6.97 us

profile of v1, /device:TPU:7, one launch (start us, length us, event | category | flops | bytes accessed | tf_op | source)
XLA Modules:
  0.0 76.3 jit_solution(2941552857206210341)
XLA Ops:
  0.6 0.0 copy-start.5
  0.6 0.0 copy-start.6
  0.7 0.0 copy-start.7
  0.7 0.6 copy-done.5
  1.3 0.0 copy-done.6
  1.3 0.0 copy-done.7
  1.3 0.0 copy-start
  1.3 0.9 %copy-done = bf16[8,1,256,64]{2,3,1,0:T(8,128)(2,1)S(1)} copy-done((bf16[8,1,256,64]{2,3,1,0:T(8,128)(2,1)S(1)}, bf16[8,1,256,64]{2,3,1,0:T(8,128)(2,1)}, u32[]{:S(2)}) %copy-start) | copy-done | bytes 262168
  2.3 0.0 copy-start.1
  2.3 1.1 %copy-done.1 = bf16[384,1024]{1,0:T(8,128)(2,1)S(1)} copy-done((bf16[384,1024]{1,0:T(8,128)(2,1)S(1)}, bf16[384,1024]{1,0:T(8,128)(2,1)}, u32[]{:S(2)}) %copy-start.1) | copy-done | bytes 786456
  3.4 0.0 copy-start.2
  3.4 1.0 %copy-done.2 = bf16[1024,256]{1,0:T(8,128)(2,1)S(1)} copy-done((bf16[1024,256]{1,0:T(8,128)(2,1)S(1)}, bf16[1024,256]{1,0:T(8,128)(2,1)}, u32[]{:S(2)}) %copy-start.2) | copy-done | bytes 524312
  4.5 0.0 copy-start.3
  4.5 0.8 copy-done.3
  5.2 0.0 copy-start.4
  5.2 0.9 %copy-done.4 = bf16[384,128]{1,0:T(8,128)(2,1)S(1)} copy-done((bf16[384,128]{1,0:T(8,128)(2,1)S(1)}, bf16[384,128]{1,0:T(8,128)(2,1)}, u32[]{:S(2)}) %copy-start.4) | copy-done | bytes 98328
  6.1 0.0 copy-start.8
  6.1 0.0 copy-start.9
  6.1 66.5 %shard_map.179 = (bf16[384,128]{1,0:T(8,128)(2,1)S(1)}, bf16[384,1024]{1,0:T(8,128)(2,1)S(1)}, f32[8,64,256]{2,1,0:T(8,128)S(1)}, f32[8,16,128]{2,1,0:T(8,128)S(1)}) custom-call(s32[12]{0:T(128)S(1)} %copy-done.5, s32[12]{0:T(128)S(1)} %copy-done.6, s32[8]{0:T(128)S(1)} %copy-done.7, bf16[384,1024]{1,0:T(8,128)(2,1)S(1)} %copy-done.1, ...), custom_call_target="tpu_custom_call" | custom-call | tf_op jit(solution)/shard_map/pallas_call | solution.py:502
  72.6 0.0 copy-done.8
  72.6 0.0 copy-done.9
  72.6 0.0 copy-start.10
  72.6 0.0 copy-start.11
  72.6 1.5 %fusion.3 = (f32[8,1,256,64]{2,3,1,0:T(8,128)}, f32[8,1,256,64]{2,3,1,0:T(8,128)}, f32[8,1,256,64]{2,3,1,0:T(8,128)}) fusion(f32[8,64,256]{2,1,0:T(8,128)S(1)} %get-tuple-element.14, f32[8,1,256,64]{2,3,1,0:T(8,128)S(1)} %copy-done.8, f32[8,1,256,64]{2,3,1,0:T(8,128)S(1)} %copy-done.9, bf16[8,1,256,64]{2,3,1,0:T(8,128)(2,1)S(1)} %copy-done), kind=kLoop, calls=%fused_computation.9 | loop fusion | flops 1703936 | bytes 3407872
  74.1 0.0 copy-done.10
  74.1 0.0 copy-done.11
  74.1 0.7 divide_subtract_fusion
  74.8 0.6 copy.28
  75.4 0.9 %copy.29 = bf16[384,1024]{1,0:T(8,128)(2,1)} copy(bf16[384,1024]{1,0:T(8,128)(2,1)S(1)} %get-tuple-element.39) | data formatting | bytes 1572864
Async XLA Ops:
  0.6 0.7 copy-start.5
  0.6 0.7 copy-start.6
  0.7 0.7 copy-start.7
  1.3 0.9 %copy-start = (bf16[8,1,256,64]{2,3,1,0:T(8,128)(2,1)S(1)}, bf16[8,1,256,64]{2,3,1,0:T(8,128)(2,1)}, u32[]{:S(2)}) copy-start(bf16[8,1,256,64]{2,3,1,0:T(8,128)(2,1)} %param.15) | copy-start | bytes 786436
  2.3 1.1 %copy-start.1 = (bf16[384,1024]{1,0:T(8,128)(2,1)S(1)}, bf16[384,1024]{1,0:T(8,128)(2,1)}, u32[]{:S(2)}) copy-start(bf16[384,1024]{1,0:T(8,128)(2,1)} %tok.1) | copy-start | bytes 2359300
  3.4 1.0 %copy-start.2 = (bf16[1024,256]{1,0:T(8,128)(2,1)S(1)}, bf16[1024,256]{1,0:T(8,128)(2,1)}, u32[]{:S(2)}) copy-start(bf16[1024,256]{1,0:T(8,128)(2,1)} %w.1) | copy-start | bytes 1572868
  4.5 0.8 copy-start.3
  5.2 0.9 %copy-start.4 = (bf16[384,128]{1,0:T(8,128)(2,1)S(1)}, bf16[384,128]{1,0:T(8,128)(2,1)}, u32[]{:S(2)}) copy-start(bf16[384,128]{1,0:T(8,128)(2,1)} %cot.1) | copy-start | bytes 294916
  6.1 66.5 %copy-start.8 = (f32[8,1,256,64]{2,3,1,0:T(8,128)S(1)}, f32[8,1,256,64]{2,3,1,0:T(8,128)}, u32[]{:S(2)}) copy-start(f32[8,1,256,64]{2,3,1,0:T(8,128)} %param.17) | copy-start | bytes 1572868
  6.1 66.5 %copy-start.9 = (f32[8,1,256,64]{2,3,1,0:T(8,128)S(1)}, f32[8,1,256,64]{2,3,1,0:T(8,128)}, u32[]{:S(2)}) copy-start(f32[8,1,256,64]{2,3,1,0:T(8,128)} %param.16) | copy-start | bytes 1572868
  72.6 1.5 %copy-start.10 = (f32[8,16,128]{2,1,0:T(8,128)S(1)}, f32[8,16,128]{2,1,0:T(8,128)}, u32[]{:S(2)}) copy-start(f32[8,16,128]{2,1,0:T(8,128)} %param.19) | copy-start | bytes 196612
  72.6 1.5 %copy-start.11 = (f32[8,16,128]{2,1,0:T(8,128)S(1)}, f32[8,16,128]{2,1,0:T(8,128)}, u32[]{:S(2)}) copy-start(f32[8,16,128]{2,1,0:T(8,128)} %param.20) | copy-start | bytes 196612

commit v2 on v1

--- a/solution.py
+++ b/solution.py
@@ -145,15 +145,19 @@
     tad,
     tlen,
     aslot,
-    tok,
-    cot,
+    tok_hbm,
+    cot_hbm,
     w,
-    down,
-    up,
+    down_hbm,
+    up_hbm,
     proj,
     tgrad,
     gdown,
     gup,
+    tok,
+    cot,
+    down,
+    up,
     wbuf,
     masked,
     sel_d,
@@ -191,6 +195,8 @@
     gd_r,
     gu_s,
     gu_r,
+    load,
+    w_load,
 ):
     z = lax.axis_index("adapter")
     m = lax.axis_index("mp")
@@ -257,50 +263,137 @@
     def grad_up_copy(src, to):
         return remote(gu_send.at[to], gu_recv.at[src], gu_s.at[to], gu_r.at[src], {"adapter": to})
 
+    loads = [
+        pltpu.make_async_copy(src, dst, load.at[i])
+        for i, (src, dst) in enumerate(
+            ((down_hbm, down), (up_hbm, up), (cot_hbm, cot), (tok_hbm, tok))
+        )
+    ]
+    w_loads = [
+        pltpu.make_async_copy(
+            w.at[:, pl.ds(h * cols, cols)], wbuf.at[z * heads + h], w_load.at[h]
+        )
+        for h in range(heads)
+    ]
+    barrier = pltpu.get_barrier_semaphore()
+    for d in range(1, na):
+        pl.semaphore_signal(
+            barrier, inc=1, device_id={"adapter": other_z(d)}, device_id_type=pl.DeviceIdType.MESH
+        )
+    for d in range(1, nm):
+        pl.semaphore_signal(
+            barrier, inc=1, device_id={"mp": other_m(d)}, device_id_type=pl.DeviceIdType.MESH
+        )
+    for copy in w_loads + loads:
+        copy.start()
+
     slot_of = [aslot[tad[i]] for i in range(na * tiles)]
+
+    def live(n):
+        row = lax.broadcasted_iota(jnp.int32, (TILE, cols), 0)
+        return jnp.where(row < tlen[z * tiles + n], 1.0, 0.0)
+
+    def send_own(h):
+        @pl.when(z < na - 1)
+        def _():
+            to_right(z * heads + h).start()
+
+        @pl.when(z > 0)
+        def _():
+            to_left(z * heads + h).start()
+
+    loads[0].wait()
+    loads[1].wait()
     for i in range(na * tiles):
         sel_d[i // tiles, i % tiles] = down[slot_of[i]]
         sel_u[i // tiles, i % tiles] = up[slot_of[i]]
-    pan_d[z] = sel_d[z]
-    pan_u[z] = sel_u[z]
-    for h in range(heads):
-        wbuf[z * heads + h] = w[:, h * cols : (h + 1) * cols]
-
-    def live(n):
-        row = lax.broadcasted_iota(jnp.int32, (TILE, cols), 0)
-        return jnp.where(row < tlen[z * tiles + n], 1.0, 0.0)
-
+    loads[2].wait()
     for n in range(tiles):
         at = slice(n * TILE, (n + 1) * TILE)
         masked[m, at] = (cot[at].astype(F32) * live(n)).astype(BF16)
-
-    barrier = pltpu.get_barrier_semaphore()
-    for d in range(1, na):
-        pl.semaphore_signal(
-            barrier, inc=1, device_id={"adapter": other_z(d)}, device_id_type=pl.DeviceIdType.MESH
-        )
-    for d in range(1, nm):
-        pl.semaphore_signal(
-            barrier, inc=1, device_id={"mp": other_m(d)}, device_id_type=pl.DeviceIdType.MESH
-        )
+    for copy in w_loads:
+        copy.wait()
     pl.semaphore_wait(barrier, na + nm - 2)
 
+    send_own(0)
     for d in range(1, na):
         panel_up(z, z, other_z(d)).start()
     for d in range(1, na):
         panel_down(z, z, other_z(d)).start()
-    for h in range(heads):
-
-        @pl.when(z < na - 1)
-        def _():
-            to_right(z * heads + h).start()
-
-        @pl.when(z > 0)
-        def _():
-            to_left(z * heads + h).start()
-
+    for h in range(1, heads):
+        send_own(h)
     for d in range(1, nm):
         mask_copy(m, other_m(d)).start()
+    pan_d[z] = sel_d[z]
+    pan_u[z] = sel_u[z]
+    loads[3].wait()
+
+    def forward(g):
+        value = dot(tok[...], wbuf[g])
+
+        @pl.when(g == m)
+        def _():
+            fro_own[...] = value
+
+        @pl.when(g != m)
+        def _():
+            fro_send[g] = value.astype(BF16)
+            frozen_copy(m, g).start()
+
+    def backward(g):
+        acc[...] += dot(masked[g], wbuf[g], NT)
+
+    def own_forward(h, carry):
+        forward(z * heads + h)
+        return carry
+
+    def own_backward(h, carry):
+        backward(z * heads + h)
+        return carry
+
+    def pass_on(t):
+        step = t // heads + 1
+        h = lax.rem(t, heads)
+        lower = (z - step) * heads + h
+        upper = (z + step) * heads + h
+
+        @pl.when(z >= step)
+        def _():
+            to_right(lower).wait_recv()
+
+            @pl.when(z < na - 1)
+            def _():
+                to_right(lower).start()
+
+        @pl.when(z + step < na)
+        def _():
+            to_left(upper).wait_recv()
+
+            @pl.when(z > 0)
+            def _():
+                to_left(upper).start()
+
+    def multiply(t):
+        step = t // heads + 1
+        h = lax.rem(t, heads)
+
+        def one(side, inner):
+            head = (z + (2 * lax.rem(side, 2) - 1) * step) * heads + h
+            valid = jnp.logical_and(head >= 0, head < na * heads)
+
+            @pl.when(jnp.logical_and(valid, side < 2))
+            def _():
+                forward(head)
+
+            @pl.when(jnp.logical_and(valid, side >= 2))
+            def _():
+                backward(head)
+
+            return inner
+
+        lax.fori_loop(0, 4, one, 0)
+
+    lax.fori_loop(0, heads, own_forward, 0)
 
     for d in range(1, na):
         panel_up(other_z(d), z, other_z(d)).wait_recv()
@@ -320,26 +413,7 @@
     for d in range(1, nm):
         sum_copy(m, other_m(d)).start()
 
-    def forward(g):
-        value = dot(tok[...], wbuf[g])
-
-        @pl.when(g == m)
-        def _():
-            fro_own[...] = value
-
-        @pl.when(g != m)
-        def _():
-            fro_send[g] = value.astype(BF16)
-            frozen_copy(m, g).start()
-
-    def backward(g):
-        acc[...] += dot(masked[g], wbuf[g], NT)
-
-    def own_forward(h, carry):
-        forward(z * heads + h)
-        return carry
-
-    lax.fori_loop(0, heads, own_forward, 0)
+    pass_on(0)
 
     total = part[pl.ds(pl.multiple_of(m * block, block), block)]
     for d in range(1, nm):
@@ -348,6 +422,11 @@
     db[pl.ds(pl.multiple_of(m * block, block), block)] = total.astype(BF16)
     for d in range(1, nm):
         rows_copy(m, other_m(d)).start()
+
+    for d in range(1, nm):
+        mask_copy(other_m(d), other_m(d)).wait_recv()
+    acc[...] = jnp.zeros_like(acc)
+    lax.fori_loop(0, heads, own_backward, 0)
     for d in range(1, nm):
         rows_copy(other_m(d), other_m(d)).wait_recv()
 
@@ -363,6 +442,8 @@
     for d in range(1, na):
         grad_down_copy(z, other_z(d)).start()
         grad_up_copy(z, other_z(d)).start()
+    if heads > 1:
+        pass_on(1)
     g_recv[z] = g_send[z]
     gu_recv[z] = gu_send[z]
     for n in range(tiles):
@@ -371,51 +452,17 @@
         down_rows, back_rows = both[:, :rank], both[:, rank:]
         term[at] = adapter_scale * dot(down_rows, up_panel(n))
         for j in range(na):
-            acc[at, j * depth : (j + 1) * depth] = dot(back_rows, pan_d[j, n])
-
-    for d in range(1, nm):
-        mask_copy(other_m(d), other_m(d)).wait_recv()
-
-    def own_backward(h, carry):
-        backward(z * heads + h)
+            acc[at, j * depth : (j + 1) * depth] += dot(back_rows, pan_d[j, n])
+
+    early = min(heads, 2)
+
+    def relay(t, carry):
+        @pl.when(t >= early)
+        def _():
+            pass_on(t)
+
+        multiply(t)
         return carry
-
-    lax.fori_loop(0, heads, own_backward, 0)
-
-    def relay(t, carry):
-        step = t // heads + 1
-        h = lax.rem(t, heads)
-        lower = (z - step) * heads + h
-        upper = (z + step) * heads + h
-
-        @pl.when(z >= step)
-        def _():
-            to_right(lower).wait_recv()
-
-            @pl.when(z < na - 1)
-            def _():
-                to_right(lower).start()
-
-        @pl.when(z + step < na)
-        def _():
-            to_left(upper).wait_recv()
-
-            @pl.when(z > 0)
-            def _():
-                to_left(upper).start()
-
-        def one(side, inner):
-            head = (z + (2 * side - 1) * step) * heads + h
-            valid = jnp.logical_and(head >= 0, head < na * heads)
-
-            @pl.when(valid)
-            def _():
-                forward(head)
-                backward(head)
-
-            return inner
-
-        return lax.fori_loop(0, 2, one, carry)
 
     lax.fori_loop(0, (na - 1) * heads, relay, 0)
 
@@ -496,6 +543,7 @@
     part = up_store.shape[1]
     down_t = jnp.swapaxes(down_store[:, 0], 1, 2)
     vmem = pl.BlockSpec(memory_space=pltpu.VMEM)
+    hbm = pl.BlockSpec(memory_space=pltpu.HBM)
     smem = pl.BlockSpec(memory_space=pltpu.SMEM)
     dma = pltpu.SemaphoreType.DMA
     sds = jax.ShapeDtypeStruct
@@ -507,9 +555,13 @@
             sds((slots, rank, depth), F32),
             sds((slots, part, cols), F32),
         ),
-        in_specs=[smem] * 3 + [vmem] * 5,
+        in_specs=[smem] * 3 + [hbm] * 5,
         out_specs=(vmem,) * 4,
         scratch_shapes=[
+            pltpu.VMEM((rows, feats), BF16),
+            pltpu.VMEM((rows, cols), BF16),
+            pltpu.VMEM((slots, rank, depth), BF16),
+            pltpu.VMEM((slots, part, cols), BF16),
             pltpu.VMEM((nm, feats, cols), BF16),
             pltpu.VMEM((nm, rows, cols), BF16),
             pltpu.VMEM((na, tiles, rank, depth), BF16),
@@ -547,9 +599,11 @@
             dma((na,)),
             dma((na,)),
             dma((na,)),
+            dma((4,)),
+            dma((value_weight.shape[1] // cols,)),
         ],
         compiler_params=pltpu.CompilerParams(
-            collective_id=0, has_side_effects=True, vmem_limit_bytes=40 * 1024 * 1024
+            collective_id=0, has_side_effects=True, vmem_limit_bytes=56 * 1024 * 1024
         ),
     )(tile_adapter, tile_length, adapter_slot, tokens, cotangent, value_weight, down_t, up_store)
     down_gradient = jnp.swapaxes(gdown, 1, 2)[:, None]

time: 76.7 us -> 70.6 us (0.920)
  local copies, waits for them, and re-layouts: 6.97 us -> 1.78 us
  Pallas kernels: 66.5 us -> 64.6 us
  other arithmetic: 2.18 us -> 3.31 us
    unnamed x26 -> x20, local copies, waits for them, and re-layouts: 6.97 us -> 1.78 us
    pallas_call x1, Pallas kernels: 66.5 us -> 64.6 us  [fused_shards(): pl.pallas_call(functools.partial(fused_kernel, na, nm), out_shape=(sds((r...]
    unnamed x1, other arithmetic: 1.49 us -> 2.62 us
where the time goes in v2:
time: 70.6 us; the launch traced here: 70.4 us
  Pallas kernels  64.6 us (92%)
  other arithmetic  3.31 us (5%)
  local copies, waits for them, and re-layouts  1.78 us (3%)
  between operations  0.75 us (1%)
    pallas_call x1, Pallas kernels, fused_shards(): pl.pallas_call(functools.partial(fused_kernel, na, nm), out_shape=(sds((r...  64.6 us
    unnamed x1, other arithmetic  2.62 us
    unnamed x20, local copies, waits for them, and re-layouts  1.78 us

profile of v2, /device:TPU:7, one launch (start us, length us, event | category | flops | bytes accessed | tf_op | source)
XLA Modules:
  0.0 70.4 jit_solution(2106037667875862711)
XLA Ops:
  0.6 0.0 copy-start
  0.6 0.0 copy-start.2
  0.7 0.0 copy-start.3
  0.7 64.6 %shard_map.179 = (bf16[384,128]{1,0:T(8,128)(2,1)}, bf16[384,1024]{1,0:T(8,128)(2,1)}, f32[8,64,256]{2,1,0:T(8,128)}, f32[8,16,128]{2,1,0:T(8,128)}) custom-call(s32[12]{0:T(128)} %tad.1, s32[12]{0:T(128)} %tlen.1, s32[8]{0:T(128)} %aslot.1, bf16[384,1024]{1,0:T(8,128)(2,1)} %tok_hbm.1, bf16[384,128]{1,0:T(8,128)(2,1)} %cot_hbm.1, bf16[1024,256]{1,0:T(8,128)(2,1)} %w.1, ...), custom_call_target="tpu_custom_call" | custom-call | tf_op jit(solution)/shard_map/pallas_call | solution.py:550
  65.2 0.0 copy-done
  65.3 0.0 copy-done.2
  65.3 0.0 copy-done.3
  65.3 0.0 copy-start.4
  65.3 0.0 copy-start.6
  65.3 0.0 copy-start.7
  65.3 0.0 copy-start.8
  65.3 0.0 copy-start.1
  65.3 2.6 %fusion.3 = (f32[8,1,256,64]{2,3,1,0:T(8,128)}, f32[8,1,256,64]{2,3,1,0:T(8,128)}, f32[8,1,256,64]{2,3,1,0:T(8,128)}) fusion(f32[8,64,256]{2,1,0:T(8,128)} %get-tuple-element.14, f32[8,1,256,64]{2,3,1,0:T(8,128)S(1)} %copy-done.2, f32[8,1,256,64]{2,3,1,0:T(8,128)S(1)} %copy-done.3, bf16[8,1,256,64]{2,3,1,0:T(8,128)(2,1)S(1)} %copy-done), kind=kLoop, calls=%fused_computation.9 | loop fusion | flops 1703936 | bytes 3407872
  67.9 0.0 copy-done.4
  67.9 0.0 copy-done.6
  67.9 0.0 copy-done.7
  68.0 0.0 copy-done.8
  68.0 0.0 copy-start.5
  68.0 0.7 divide_subtract_fusion
  68.7 0.2 copy-done.5
  68.9 0.6 copy.28
  69.5 0.0 copy-done.1
  69.5 0.9 %copy.29 = bf16[384,1024]{1,0:T(8,128)(2,1)} copy(bf16[384,1024]{1,0:T(8,128)(2,1)S(1)} %copy-done.1) | data formatting | bytes 1572864
Async XLA Ops:
  0.6 64.6 %copy-start = (bf16[8,1,256,64]{2,3,1,0:T(8,128)(2,1)S(1)}, bf16[8,1,256,64]{2,3,1,0:T(8,128)(2,1)}, u32[]{:S(2)}) copy-start(bf16[8,1,256,64]{2,3,1,0:T(8,128)(2,1)} %param.15) | copy-start | bytes 786436
  0.6 64.6 %copy-start.2 = (f32[8,1,256,64]{2,3,1,0:T(8,128)S(1)}, f32[8,1,256,64]{2,3,1,0:T(8,128)}, u32[]{:S(2)}) copy-start(f32[8,1,256,64]{2,3,1,0:T(8,128)} %param.17) | copy-start | bytes 1572868
  0.7 64.6 %copy-start.3 = (f32[8,1,256,64]{2,3,1,0:T(8,128)S(1)}, f32[8,1,256,64]{2,3,1,0:T(8,128)}, u32[]{:S(2)}) copy-start(f32[8,1,256,64]{2,3,1,0:T(8,128)} %param.16) | copy-start | bytes 1572868
  65.3 2.7 %copy-start.4 = (bf16[8,16,128]{2,1,0:T(8,128)(2,1)S(1)}, bf16[8,16,128]{2,1,0:T(8,128)(2,1)}, u32[]{:S(2)}) copy-start(bf16[8,16,128]{2,1,0:T(8,128)(2,1)} %up_hbm.1) | copy-start | bytes 98308
  65.3 2.7 %copy-start.6 = (f32[8,16,128]{2,1,0:T(8,128)S(1)}, f32[8,16,128]{2,1,0:T(8,128)}, u32[]{:S(2)}) copy-start(f32[8,16,128]{2,1,0:T(8,128)} %param.19) | copy-start | bytes 196612
  65.3 2.7 %copy-start.7 = (f32[8,16,128]{2,1,0:T(8,128)S(1)}, f32[8,16,128]{2,1,0:T(8,128)}, u32[]{:S(2)}) copy-start(f32[8,16,128]{2,1,0:T(8,128)} %param.20) | copy-start | bytes 196612
  65.3 2.6 %copy-start.8 = (f32[8,16,128]{2,1,0:T(8,128)S(1)}, f32[8,16,128]{2,1,0:T(8,128)}, u32[]{:S(2)}) copy-start(f32[8,16,128]{2,1,0:T(8,128)} %get-tuple-element.15) | copy-start | bytes 196612
  65.3 4.2 %copy-start.1 = (bf16[384,1024]{1,0:T(8,128)(2,1)S(1)}, bf16[384,1024]{1,0:T(8,128)(2,1)}, u32[]{:S(2)}) copy-start(bf16[384,1024]{1,0:T(8,128)(2,1)} %get-tuple-element.39) | copy-start | bytes 2359300
  68.0 0.9 %copy-start.5 = (bf16[384,128]{1,0:T(8,128)(2,1)S(1)}, bf16[384,128]{1,0:T(8,128)(2,1)}, u32[]{:S(2)}) copy-start(bf16[384,128]{1,0:T(8,128)(2,1)} %get-tuple-element.38) | copy-start | bytes 294916

commit v3 on v2

--- a/solution.py
+++ b/solution.py
@@ -302,26 +302,26 @@
         def _():
             to_left(z * heads + h).start()
 
+    for copy in w_loads:
+        copy.wait()
+    pl.semaphore_wait(barrier, na + nm - 2)
+    send_own(0)
+
     loads[0].wait()
     loads[1].wait()
     for i in range(na * tiles):
         sel_d[i // tiles, i % tiles] = down[slot_of[i]]
         sel_u[i // tiles, i % tiles] = up[slot_of[i]]
-    loads[2].wait()
-    for n in range(tiles):
-        at = slice(n * TILE, (n + 1) * TILE)
-        masked[m, at] = (cot[at].astype(F32) * live(n)).astype(BF16)
-    for copy in w_loads:
-        copy.wait()
-    pl.semaphore_wait(barrier, na + nm - 2)
-
-    send_own(0)
     for d in range(1, na):
         panel_up(z, z, other_z(d)).start()
     for d in range(1, na):
         panel_down(z, z, other_z(d)).start()
     for h in range(1, heads):
         send_own(h)
+    loads[2].wait()
+    for n in range(tiles):
+        at = slice(n * TILE, (n + 1) * TILE)
+        masked[m, at] = (cot[at].astype(F32) * live(n)).astype(BF16)
     for d in range(1, nm):
         mask_copy(m, other_m(d)).start()
     pan_d[z] = sel_d[z]
@@ -394,6 +394,7 @@
         lax.fori_loop(0, 4, one, 0)
 
     lax.fori_loop(0, heads, own_forward, 0)
+    pass_on(0)
 
     for d in range(1, na):
         panel_up(other_z(d), z, other_z(d)).wait_recv()
@@ -412,8 +413,6 @@
         part[at] = jnp.concatenate([down_part, back_part], axis=1)
     for d in range(1, nm):
         sum_copy(m, other_m(d)).start()
-
-    pass_on(0)
 
     total = part[pl.ds(pl.multiple_of(m * block, block), block)]
     for d in range(1, nm):
@@ -454,6 +453,24 @@
         for j in range(na):
             acc[at, j * depth : (j + 1) * depth] += dot(back_rows, pan_d[j, n])
 
+    def sum_slots():
+        for d in range(1, na):
+            grad_down_copy(other_z(d), other_z(d)).wait_recv()
+            grad_up_copy(other_z(d), other_z(d)).wait_recv()
+
+        def slot_sum(s, inner):
+            total_d = jnp.zeros((rank, depth), F32)
+            total_u = jnp.zeros((rank_part, cols), F32)
+            for i in range(na * tiles):
+                use = jnp.where(slot_of[i] == s, 1.0, 0.0)
+                total_d += use * g_recv[i // tiles, i % tiles].astype(F32)
+                total_u += use * gu_recv[i // tiles, i % tiles]
+            gdown[s] = total_d
+            gup[s] = total_u
+            return inner
+
+        lax.fori_loop(0, slots, slot_sum, 0)
+
     early = min(heads, 2)
 
     def relay(t, carry):
@@ -464,24 +481,10 @@
         multiply(t)
         return carry
 
-    lax.fori_loop(0, (na - 1) * heads, relay, 0)
-
-    for d in range(1, na):
-        grad_down_copy(other_z(d), other_z(d)).wait_recv()
-        grad_up_copy(other_z(d), other_z(d)).wait_recv()
-
-    def slot_sum(s, carry):
-        total_d = jnp.zeros((rank, depth), F32)
-        total_u = jnp.zeros((rank_part, cols), F32)
-        for i in range(na * tiles):
-            use = jnp.where(slot_of[i] == s, 1.0, 0.0)
-            total_d += use * g_recv[i // tiles, i % tiles].astype(F32)
-            total_u += use * gu_recv[i // tiles, i % tiles]
-        gdown[s] = total_d
-        gup[s] = total_u
-        return carry
-
-    lax.fori_loop(0, slots, slot_sum, 0)
+    lax.fori_loop(0, (na - 1) * heads - 1, relay, 0)
+    sum_slots()
+    lax.fori_loop((na - 1) * heads - 1, (na - 1) * heads, relay, 0)
+
     tgrad[...] = acc[...].astype(BF16)
 
     for d in range(1, nm):
@@ -518,6 +521,18 @@
         return carry
 
     lax.fori_loop(0, na * heads, drain, 0)
+
+
+def finish_kernel(proj, tgrad, gdown, gup, down, df, dsec, up, uf, us, *outs):
+    outs[0][...] = proj[...]
+    outs[1][...] = tgrad[...]
+    for i, (store, first, second, grad) in enumerate(
+        ((down, df, dsec, gdown), (up, uf, us, gup))
+    ):
+        for s in range(store.shape[0]):
+            values = adam_step(store[s], first[s], second[s], grad[s])
+            for k, value in enumerate(values):
+                outs[2 + 3 * i + k][s] = value
 
 
 def fused_shards(
@@ -606,13 +621,22 @@
             collective_id=0, has_side_effects=True, vmem_limit_bytes=56 * 1024 * 1024
         ),
     )(tile_adapter, tile_length, adapter_slot, tokens, cotangent, value_weight, down_t, up_store)
-    down_gradient = jnp.swapaxes(gdown, 1, 2)[:, None]
-    return (
-        proj,
-        tgrad,
-        *adam_step(down_store, down_first, down_second, down_gradient),
-        *adam_step(up_store, up_first, up_second, gup),
-    )
+    first_t = jnp.swapaxes(down_first[:, 0], 1, 2)
+    second_t = jnp.swapaxes(down_second[:, 0], 1, 2)
+    outs = pl.pallas_call(
+        finish_kernel,
+        out_shape=(
+            sds((rows, cols), BF16),
+            sds((rows, feats), BF16),
+            *[sds((slots, rank, depth), F32)] * 3,
+            *[sds((slots, part, cols), F32)] * 3,
+        ),
+        in_specs=[vmem] * 10,
+        out_specs=(vmem,) * 8,
+        compiler_params=pltpu.CompilerParams(vmem_limit_bytes=60 * 1024 * 1024),
+    )(proj, tgrad, gdown, gup, down_t, first_t, second_t, up_store, up_first, up_second)
+    back = [jnp.swapaxes(a, 1, 2)[:, None] for a in outs[2:5]]
+    return (*outs[:2], *back, *outs[5:])
 
 
 def by_share(na, nm, *arrays):

time: 70.6 us -> 68.9 us (0.976)
  Pallas kernels: 64.6 us -> 68 us
  other arithmetic: 3.31 us -> 0 us
  local copies, waits for them, and re-layouts: 1.78 us -> 0 us
    pallas_call x0 -> x1, Pallas kernels: none -> 3.57 us  [fused_shards(): pl.pallas_call(finish_kernel, out_shape=(sds((rows, cols), BF16), sds((ro...]
    unnamed x1 -> x0, other arithmetic: 2.62 us -> none
    unnamed x20 -> x0, local copies, waits for them, and re-layouts: 1.78 us -> none
where the time goes in v3:
time: 68.9 us; the launch traced here: 68.7 us
  Pallas kernels  68 us (99%)
    pallas_call x1, Pallas kernels, fused_shards(): pl.pallas_call(functools.partial(fused_kernel, na, nm), out_shape=(sds((r...  64.5 us
    pallas_call x1, Pallas kernels, fused_shards(): pl.pallas_call(finish_kernel, out_shape=(sds((rows, cols), BF16), sds((ro...  3.57 us

profile of v3, /device:TPU:7, one launch (start us, length us, event | category | flops | bytes accessed | tf_op | source)
XLA Modules:
  0.0 68.7 jit_solution(15521001880447722207)
XLA Ops:
  0.6 64.5 %shard_map.179 = (bf16[384,128]{1,0:T(8,128)(2,1)}, bf16[384,1024]{1,0:T(8,128)(2,1)}, f32[8,64,256]{2,1,0:T(8,128)}, f32[8,16,128]{2,1,0:T(8,128)}) custom-call(s32[12]{0:T(128)} %tad.1, s32[12]{0:T(128)} %tlen.1, s32[8]{0:T(128)} %aslot.1, bf16[384,1024]{1,0:T(8,128)(2,1)} %tok_hbm.1, bf16[384,128]{1,0:T(8,128)(2,1)} %cot_hbm.1, bf16[1024,256]{1,0:T(8,128)(2,1)} %w.1, ...), custom_call_target="tpu_custom_call" | custom-call | tf_op jit(solution)/shard_map/pallas_call | solution.py:565
  65.1 3.6 %shard_map.180 = (bf16[384,128]{1,0:T(8,128)(2,1)}, bf16[384,1024]{1,0:T(8,128)(2,1)}, f32[8,64,256]{2,1,0:T(8,128)}, f32[8,64,256]{2,1,0:T(8,128)}, f32[8,64,25...) custom-call(bf16[384,128]{1,0:T(8,128)(2,1)} %get-tuple-element.20.proj, ...), custom_call_target="tpu_custom_call" | custom-call | tf_op jit(solution)/shard_map/pallas_call | solution.py:626

commit v4 on v3

--- a/solution.py
+++ b/solution.py
@@ -438,9 +438,6 @@
         for j in range(na):
             g_send[j, n] = g_tile[:, j * depth : (j + 1) * depth].astype(BF16)
             gu_send[j, n] = gu_tile[j * rank_part : (j + 1) * rank_part]
-    for d in range(1, na):
-        grad_down_copy(z, other_z(d)).start()
-        grad_up_copy(z, other_z(d)).start()
     if heads > 1:
         pass_on(1)
     g_recv[z] = g_send[z]
@@ -478,12 +475,18 @@
         def _():
             pass_on(t)
 
+        @pl.when(t == last_forward)
+        def _():
+            for d in range(1, na):
+                grad_down_copy(z, other_z(d)).start()
+                grad_up_copy(z, other_z(d)).start()
+
         multiply(t)
         return carry
 
-    lax.fori_loop(0, (na - 1) * heads - 1, relay, 0)
+    last_forward = max((na - 2) * heads - 1, 0)
+    lax.fori_loop(0, (na - 1) * heads, relay, 0)
     sum_slots()
-    lax.fori_loop((na - 1) * heads - 1, (na - 1) * heads, relay, 0)
 
     tgrad[...] = acc[...].astype(BF16)
 

time: 68.9 us -> 66.1 us (0.959)
  Pallas kernels: 68 us -> 65.2 us
    pallas_call x1, Pallas kernels: 64.5 us -> 61.7 us  [fused_shards(): pl.pallas_call(functools.partial(fused_kernel, na, nm), out_shape=(sds((r...]
where the time goes in v4:
time: 66.1 us; the launch traced here: 65.9 us
  Pallas kernels  65.2 us (99%)
    pallas_call x1, Pallas kernels, fused_shards(): pl.pallas_call(functools.partial(fused_kernel, na, nm), out_shape=(sds((r...  61.7 us
    pallas_call x1, Pallas kernels, fused_shards(): pl.pallas_call(finish_kernel, out_shape=(sds((rows, cols), BF16), sds((ro...  3.57 us

profile of v4, /device:TPU:7, one launch (start us, length us, event | category | flops | bytes accessed | tf_op | source)
XLA Modules:
  0.0 65.9 jit_solution(4000890646817668989)
XLA Ops:
  0.6 61.7 %shard_map.179 = (bf16[384,128]{1,0:T(8,128)(2,1)}, bf16[384,1024]{1,0:T(8,128)(2,1)}, f32[8,64,256]{2,1,0:T(8,128)}, f32[8,16,128]{2,1,0:T(8,128)}) custom-call(s32[12]{0:T(128)} %tad.1, s32[12]{0:T(128)} %tlen.1, s32[8]{0:T(128)} %aslot.1, bf16[384,1024]{1,0:T(8,128)(2,1)} %tok_hbm.1, bf16[384,128]{1,0:T(8,128)(2,1)} %cot_hbm.1, bf16[1024,256]{1,0:T(8,128)(2,1)} %w.1, ...), custom_call_target="tpu_custom_call" | custom-call | tf_op jit(solution)/shard_map/pallas_call | solution.py:568
  62.3 3.6 %shard_map.180 = (bf16[384,128]{1,0:T(8,128)(2,1)}, bf16[384,1024]{1,0:T(8,128)(2,1)}, f32[8,64,256]{2,1,0:T(8,128)}, f32[8,64,256]{2,1,0:T(8,128)}, f32[8,64,25...) custom-call(bf16[384,128]{1,0:T(8,128)(2,1)} %get-tuple-element.20.proj, ...), custom_call_target="tpu_custom_call" | custom-call | tf_op jit(solution)/shard_map/pallas_call | solution.py:629
